TPU v7x, 32 devices: a whole 2x2x4 slice. The times are simulated.
32 devices in a mesh: seq: 8 (over z, x), head: 4 (over y, core).
Axes of the slice: x: 2, y: 2, z: 4, core: 2. Of those that a mesh axis runs over, the one named last changes fastest.
Arguments:
- query_rows: bfloat16 [4096, 4096], P('seq', 'head'), may hold values from -6 to 6
- key_rows: bfloat16 [4096, 4096], P('seq', 'head'), may hold values from -6 to 6
- value_rows: bfloat16 [4096, 4096], P('seq', 'head'), may hold values from -19 to 19
- norm_gain: float32 [4096], P('head'), may hold values from 0.5 to 1.5
- out_grad: bfloat16 [4096, 4096], P('seq', 'head'), may hold values from -6 to 6
Outputs:
- attn_out: bfloat16 [4096, 4096], P('seq', 'head')
- grad_query: bfloat16 [4096, 4096], P('seq', 'head')
- grad_key: bfloat16 [4096, 4096], P('seq', 'head')
- grad_value: bfloat16 [4096, 4096], P('seq', 'head')
- grad_gain: float32 [4096], P('head')
All inputs are finite; a program needn't handle non-finite values.
Results may differ from a plain program's by a relative error of at most 0.0059.
Values sent between devices are 32-bit elements; how exact they have to be, the bound alone decides.
A program may use at most 128 MiB of HBM per device.

v0:
```python
import jax
import jax.numpy as jnp
from jax import lax
from jax.sharding import PartitionSpec as P

HEADS = 32
DH = 128


norm_eps = 1e-06


def prefix_2(array, axis, combine, identity, reverse):
    peers, mine = (lax.axis_size(axis), lax.axis_index(axis))
    everything = lax.all_gather(array, axis)
    start = jnp.broadcast_to(jnp.asarray(identity, array.dtype), array.shape)

    def hop(k, before):
        at = peers - 1 - k if reverse else k
        reached = at > mine if reverse else at < mine
        new = combine(before, everything[at])
        return jnp.where(reached, new, before)

    return lax.fori_loop(0, peers, hop, start)


def add_states(earlier, later):
    return earlier + later


def head_major(rows, local_heads):
    return rows.reshape(rows.shape[0], local_heads, DH).transpose(1, 0, 2)


def row_major(heads_first):
    return heads_first.transpose(1, 0, 2).reshape(
        heads_first.shape[1], heads_first.shape[0] * heads_first.shape[2]
    )


def body(query_rows, key_rows, value_rows, norm_gain, out_grad):
    tok_rows = query_rows.shape[0]
    full_width = query_rows.shape[1]
    local_heads = full_width // DH
    columns = HEADS * DH
    query_heads = head_major(query_rows, local_heads)
    key_heads = head_major(key_rows, local_heads)
    value_heads = head_major(value_rows, local_heads)
    own_state = jnp.einsum(
        "hti,htj->hij", key_heads, value_heads, preferred_element_type=jnp.float32
    )
    zero_state = jnp.zeros_like(own_state)
    prefix = prefix_2(own_state, "seq", add_states, zero_state, False)
    prefix_bf = prefix.astype(jnp.bfloat16)
    causal = jnp.tril(jnp.ones((tok_rows, tok_rows), dtype=bool))[None, :, :]
    scores = jnp.einsum("htd,hsd->hts", query_heads, key_heads, preferred_element_type=jnp.float32)
    scores_bf = jnp.where(causal, scores, 0.0).astype(jnp.bfloat16)
    left_side = jnp.concatenate([query_heads, scores_bf], axis=2)
    right_side = jnp.concatenate([prefix_bf, value_heads], axis=1)
    attention = jnp.einsum(
        "htk,hkj->htj", left_side, right_side, preferred_element_type=jnp.float32
    )
    attention = row_major(attention)
    grad_wide = out_grad.astype(jnp.float32)
    scaled = grad_wide * norm_gain
    square_sum, dot_sum = lax.psum(
        (jnp.sum(attention * attention, axis=1), jnp.sum(scaled * attention, axis=1)), "head"
    )
    inverse = lax.rsqrt(square_sum / columns + norm_eps)
    normed = attention * inverse[:, None]
    attn_out = (normed * norm_gain).astype(jnp.bfloat16)
    gain_part = jnp.sum(grad_wide * normed, axis=0)
    dot_mean = dot_sum * inverse / columns
    grad_attn = (inverse[:, None] * (scaled - normed * dot_mean[:, None])).astype(jnp.bfloat16)
    grad_heads = head_major(grad_attn, local_heads)
    dscores = jnp.einsum(
        "htj,hsj->hts", grad_heads, value_heads, preferred_element_type=jnp.float32
    )
    dscores_bf = jnp.where(causal, dscores, 0.0).astype(jnp.bfloat16)
    own_grad = jnp.einsum(
        "hti,htj->hij", query_heads, grad_heads, preferred_element_type=jnp.float32
    )
    suffix = prefix_2(own_grad, "seq", add_states, zero_state, True)
    grad_gain = lax.psum(gain_part, "seq")
    suffix_bf = suffix.astype(jnp.bfloat16)
    grad_query = jnp.einsum(
        "htj,hij->hti", grad_heads, prefix_bf, preferred_element_type=jnp.float32
    )
    grad_query = grad_query + jnp.einsum(
        "hts,hsi->hti", dscores_bf, key_heads, preferred_element_type=jnp.float32
    )
    key_left = jnp.concatenate([value_heads, dscores_bf.transpose(0, 2, 1)], axis=2)
    key_right = jnp.concatenate([suffix_bf.transpose(0, 2, 1), query_heads], axis=1)
    grad_key = jnp.einsum("hsk,hki->hsi", key_left, key_right, preferred_element_type=jnp.float32)
    value_left = jnp.concatenate([key_heads, scores_bf.transpose(0, 2, 1)], axis=2)
    value_right = jnp.concatenate([suffix_bf, grad_heads], axis=1)
    grad_value = jnp.einsum(
        "hsk,hkj->hsj", value_left, value_right, preferred_element_type=jnp.float32
    )
    grad_query = row_major(grad_query).astype(jnp.bfloat16)
    grad_key = row_major(grad_key).astype(jnp.bfloat16)
    grad_value = row_major(grad_value).astype(jnp.bfloat16)
    return (attn_out, grad_query, grad_key, grad_value, grad_gain)


def solution(mesh):
    in_specs = (P("seq", "head"), P("seq", "head"), P("seq", "head"), P("head"), P("seq", "head"))
    out_specs = (P("seq", "head"), P("seq", "head"), P("seq", "head"), P("seq", "head"), P("head"))
    return jax.shard_map(body, mesh=mesh, in_specs=in_specs, out_specs=out_specs, check_vma=False)
```

profile of v0, /device:TPU:0, one launch (start us, length us, event | category | flops | bytes accessed | tf_op | source)
XLA Modules:
  0.0 228.1 jit_solution(489990412108936092)
XLA Ops:
  7.2 1.5 copy.37
  8.7 1.9 copy.41
  10.6 1.2 fusion.44
  11.9 2.3 copy.36
  14.2 4.5 %fusion.43 = bf16[8,512,512]{2,1,0:T(8,128)(2,1)} fusion(bf16[8,512,128]{1,2,0:T(8,128)(2,1)} %bitcast.72, bf16[8,512,128]{1,2,0:T(8,128)(2,1)S(1)} %bitcast.69), kind=kOutput, calls=%fused_computation.55 | convolution fusion | flops 536870912 | bytes 6291456 | tf_op jit(solution)/shard_map/htd,hsd->hts/dot_general | solution.py:56
  18.7 6.5 %copy.40 = bf16[8,512,512]{1,2,0:T(8,128)(2,1)} copy(bf16[8,512,512]{2,1,0:T(8,128)(2,1)} %fusion.43) | data formatting | bytes 8388608 | tf_op jit(solution)/shard_map/htd,hsd->hts/dot_general | solution.py:56
  25.3 0.7 copy-done.4
  26.0 5.1 %select_convert_fusion.1 = bf16[8,512,512]{1,2,0:T(8,128)(2,1)} fusion(bf16[8,512,512]{1,2,0:T(8,128)(2,1)} %copy.40, pred[512,512]{0,1:T(8,128)(4,1)S(1)} %iota_compare_fusion.1), kind=kLoop, calls=%fused_computation.7 | loop fusion | flops 2097152 | bytes 8650752 | tf_op jit(solution)/shard_map/convert_element_type | solution.py:57
  31.1 57.0 %all-gather.5.cloned.1.call-done = f32[64,128,128]{2,1,0:T(8,128)} async-done(((f32[8,128,128]{2,1,0:T(8,128)}), f32[64,128,128]{2,1,0:T(8,128)}) %all-gather.5.cloned.1.call-update) | async-done | bytes 4194320 | tf_op jit(solution)/shard_map/all_gather | solution.py:15
  88.1 10.1 %while.30 = (s32[]{:T(128)}, f32[8,128,128]{2,1,0:T(8,128)S(1)}, s32[]{:T(128)}, f32[8,8,128,128]{3,2,1,0:T(8,128)}, s32[]{:T(128)}, /*index=5*/s32[]{:T(128)}) while((s32[]{:T(128)}, f32[8,128,128]{2,1,0:T(8,128)S(1)}, s32[]{:T(128)}, f32[8,8,128,128]{3,2,1,0:T(8,128)}, s32[]{:T(128)}, /*index=5*/s32[]{:T(128)}) %tuple.90), condition=%wide.region_1.2_spmd.clone, body=%wide.region_0.1_spmd.clone.sunk | while | flops 393220 | bytes 1572965 | solution.py:24
  88.1 1.3 add_select_fusion.4
  89.5 1.2 add_select_fusion.4
  90.7 1.2 add_select_fusion.4
  92.0 1.2 add_select_fusion.4
  93.2 1.2 add_select_fusion.4
  94.5 1.2 add_select_fusion.4
  95.7 1.2 add_select_fusion.4
  97.0 1.2 add_select_fusion.4
  98.4 4.5 %fusion.23 = (f32[512]{0:T(512)S(1)}, f32[8,512,128]{1,2,0:T(8,128)}) fusion(bf16[8,512,512]{1,2,0:T(8,128)(2,1)} %select_convert_fusion.1, bf16[8,512,128]{1,2,0:T(8,128)(2,1)S(1)} %bitcast.73, bf16[8,512,128]{1,2,0:T(8,128)(2,1)S(1)} %bitcast.65, bf16[8,128,128]{1,2,0:T(8,128)(2,1)S(1)} %copy.43), kind=kOutput, calls=%fused_computation.32 | convolution fusion | flops 685243904 | bytes 8652800 | tf_op jit(solution)/shard_map/htk,hkj->htj/dot_general | solution.py:60
  102.9 5.8 %psum.21 = f32[512]{0:T(512)S(1)} all-reduce(f32[512]{0:T(512)S(1)} %get-tuple-element.262), channel_id=1, replica_groups=mesh['seq'=8,'head'=4] {'head'}, use_global_device_ids=true, to_apply=%region_3.4 | all-reduce | flops 512 | bytes 4096 | tf_op jit(solution)/shard_map/psum | solution.py:66
  108.7 1.9 copy.45
  110.6 1.9 fusion.22
  112.6 6.6 %psum.22 = f32[512]{0:T(512)S(1)} all-reduce(f32[512]{0:T(512)S(1)} %get-tuple-element.241), channel_id=1, replica_groups=mesh['seq'=8,'head'=4] {'head'}, use_global_device_ids=true, to_apply=%region_5.6 | all-reduce | flops 512 | bytes 4096 | tf_op jit(solution)/shard_map/psum | solution.py:66
  119.2 3.1 %fusion.21 = (bf16[512,1024]{1,0:T(8,128)(2,1)}, bf16[512,1024]{1,0:T(8,128)(2,1)}) fusion(bf16[512,1024]{1,0:T(8,128)(2,1)} %param.13, f32[512,1024]{1,0:T(8,128)S(1)} %copy.45, f32[512]{0:T(512)S(1)} %multiply_multiply_fusion, f32[1024]{0:T(1024)S(1)} %copy-done.6, f32[512]{0:T(512)S(1)} %add_rsqrt_fusion), kind=kLoop, calls=%fused_computation.29 | loop fusion | flops 4718592 | bytes 5251072 | tf_op jit(solution)/shard_map/convert_element_type | solution.py:74
  122.3 1.6 copy.47
  123.9 1.2 convolution_bitcast_fusion
  125.1 2.1 copy.55
  127.3 7.4 %fusion = (bf16[8,512,512]{1,2,0:T(8,128)(2,1)}, bf16[8,512,512]{1,2,0:T(8,128)(2,1)}, bf16[8,512,512]{2,1,0:T(8,128)(2,1)}) fusion(bf16[8,512,512]{2,1,0:T(8,128)(2,1)} %fusion.43, pred[512,512]{0,1:T(8,128)(4,1)S(1)} %iota_compare_fusion, bf16[8,512,128]{1,2,0:T(8,128)(2,1)S(1)} %bitcast.61, bf16[8,512,128]{1,2,0:T(8,128)(2,1)S(1)} %bitcast.66), kind=kOutput, calls=%fused_computation.3 | convolution fusion | flops 541065216 | bytes 19136512 | tf_op jit(solution)/shard_map/htj,hsj->hts/dot_general | solution.py:76
  134.8 6.5 %copy.52 = bf16[8,512,512]{1,2,0:T(8,128)(2,1)} copy(bf16[8,512,512]{2,1,0:T(8,128)(2,1)} %get-tuple-element.264) | data formatting | bytes 8388608 | tf_op jit(solution)/shard_map/htj,hsj->hts/dot_general | solution.py:76
  141.3 3.3 %fusion.14 = f32[8,512,128]{1,2,0:T(8,128)S(1)} fusion(bf16[8,512,128]{1,2,0:T(8,128)(2,1)} %bitcast.70, bf16[8,512,512]{1,2,0:T(8,128)(2,1)} %copy.52, pred[512,512]{0,1:T(8,128)(4,1)S(1)} %copy-done.5), kind=kOutput, calls=%fused_computation.20 | convolution fusion | flops 538968064 | bytes 7602176 | tf_op jit(solution)/shard_map/hts,hsi->hti/dot_general | solution.py:89
  144.6 1.5 add_convert_fusion
  146.0 2.3 copy.59
  148.3 20.4 %psum.23 = f32[1024]{0:T(1024)} all-reduce(f32[1024]{0:T(1024)S(1)} %get-tuple-element.240), channel_id=1, replica_groups=mesh['seq'=8,'head'=4] {'seq'}, use_global_device_ids=true, to_apply=%region_9.10 | all-reduce | flops 1024 | bytes 8192 | tf_op jit(solution)/shard_map/psum | solution.py:84
  168.7 30.1 %all-gather.7.cloned.1.call-done = f32[64,128,128]{2,1,0:T(8,128)} async-done(((f32[8,128,128]{2,1,0:T(8,128)}), f32[64,128,128]{2,1,0:T(8,128)}) %all-gather.7.cloned.1.call-update) | async-done | bytes 4194320 | tf_op jit(solution)/shard_map/all_gather | solution.py:15
  198.8 10.0 %while.31 = (s32[]{:T(128)}, f32[8,128,128]{2,1,0:T(8,128)S(1)}, s32[]{:T(128)}, f32[8,8,128,128]{3,2,1,0:T(8,128)}, s32[]{:T(128)}, /*index=5*/s32[]{:T(128)}, s32[]{:T(128)}, s32[]{:T(128)}) while((s32[]{:T(128)}, f32[8,128,128]{2,1,0:T(8,128)S(1)}, s32[]{:T(128)}, f32[8,8,128,128]{3,2,1,0:T(8,128)}, s32[]{:T(128)}, ...), condition=%wide.region_7.8_spmd.clone, body=%wide.region_6.7_spmd.clone.sunk | while | flops 393224 | bytes 1573027 | solution.py:24
  198.8 1.2 add_select_fusion.5
  200.1 1.2 add_select_fusion.5
  201.3 1.2 add_select_fusion.5
  202.6 1.2 add_select_fusion.5
  203.8 1.2 add_select_fusion.5
  205.1 1.2 add_select_fusion.5
  206.4 1.2 add_select_fusion.5
  207.6 1.2 add_select_fusion.5
  208.9 0.9 copy.57
  209.8 4.7 %fusion.24 = bf16[8,512,128]{1,2,0:T(8,128)(2,1)} fusion(bf16[8,512,512]{1,2,0:T(8,128)(2,1)} %get-tuple-element.260, bf16[8,512,128]{1,2,0:T(8,128)(2,1)} %bitcast.71, bf16[8,512,128]{1,2,0:T(8,128)(2,1)S(1)} %bitcast.63, bf16[8,128,128]{1,2,0:T(8,128)(2,1)} %copy.57), kind=kOutput, calls=%fused_computation.35 | convolution fusion | flops 684720128 | bytes 7602176 | tf_op jit(solution)/shard_map/hsk,hkj->hsj/dot_general | solution.py:97
  214.5 2.3 copy.61
  216.7 3.2 %fusion.27 = bf16[8,512,128]{1,2,0:T(8,128)(2,1)S(1)} fusion(bf16[8,512,512]{1,2,0:T(8,128)(2,1)} %get-tuple-element.261, bf16[8,512,128]{1,2,0:T(8,128)(2,1)S(1)} %bitcast.67, bf16[8,512,128]{1,2,0:T(8,128)(2,1)S(1)} %bitcast.75, bf16[8,128,128]{1,2,0:T(8,128)(2,1)S(1)} %convert_bitcast_fusion), kind=kOutput, calls=%fused_computation.36 | convolution fusion | flops 684720128 | bytes 7602176 | tf_op jit(solution)/shard_map/hsk,hki->hsi/dot_general | solution.py:94
  219.9 1.3 copy.60
  (26 shorter events, 0.6 us)
Async XLA Ops:
  7.2 80.9 %all-gather.5.cloned.1.call-start = ((), (), s32[]{:S(2)}) async-start(), calls=%async_computation | async-start | bytes 4718592 | tf_op jit(solution)/shard_map/all_gather | solution.py:15
  8.7 5.5 %copy-start = (bf16[512,1024]{0,1:T(8,128)(2,1)}, bf16[512,1024]{0,1:T(8,128)(2,1)S(1)}, u32[]{:S(2)}) copy-start(bf16[512,1024]{0,1:T(8,128)(2,1)S(1)} %copy.37) | copy-start | bytes 3145732
  11.9 187.0 %all-gather.7.cloned.1.call-start = ((), (), s32[]{:S(2)}) async-start(), calls=%async_computation.1 | async-start | bytes 4718592 | tf_op jit(solution)/shard_map/all_gather | solution.py:15
  25.3 0.7 copy-start.4
  88.1 10.3 %copy-start.1 = (bf16[512,1024]{0,1:T(8,128)(2,1)S(1)}, bf16[512,1024]{0,1:T(8,128)(2,1)}, u32[]{:S(2)}) copy-start(bf16[512,1024]{0,1:T(8,128)(2,1)} %copy.36) | copy-start | bytes 3145732
  102.9 7.7 %copy-start.6 = (f32[1024]{0:T(1024)S(1)}, f32[1024]{0:T(1024)}, u32[]{:S(2)}) copy-start(f32[1024]{0:T(1024)} %param.12) | copy-start | bytes 12292
  122.3 1.6 copy-start.2
  134.8 6.5 %copy-start.5 = (pred[512,512]{0,1:T(8,128)(4,1)S(1)}, pred[512,512]{0,1:T(8,128)(4,1)}, u32[]{:S(2)}) copy-start(pred[512,512]{0,1:T(8,128)(4,1)} %copy-done.4) | copy-start | bytes 786436
  209.8 7.0 %copy-start.3 = (bf16[512,1024]{0,1:T(8,128)(2,1)S(1)}, bf16[512,1024]{0,1:T(8,128)(2,1)}, u32[]{:S(2)}) copy-start(bf16[512,1024]{0,1:T(8,128)(2,1)} %copy.36) | copy-start | bytes 3145732
Sparse Core Ops, SparseCore 0:
  12.0 76.0 all-gather.4
  127.3 71.4 all-gather.6
where the time goes:
time: 230 us; the launch traced here: 228 us
  waiting for transfers between devices  87.1 us (38%)
  blocking collectives  32.8 us (14%)
  local copies, waits for them, and re-layouts  31.8 us (14%)
  matrix products  31.5 us (14%)
  other arithmetic  30.1 us (13%)
  between operations  14.2 us (6%)
    all_gather x2, waiting for transfers between devices, prefix_2(): everything = lax.all_gather(array, axis)  87.1 us
    psum x1, blocking collectives, body(): grad_gain = lax.psum(gain_part, 'seq')  20.4 us
    select_n x16, other arithmetic, hop(): return jnp.where(reached, new, before)  19.7 us
    psum x2, blocking collectives, body(): lax.psum((jnp.sum(attention * attention, axis=1), jnp.sum(scaled * attent...  12.4 us
    unnamed x20, local copies, waits for them, and re-layouts  12.2 us
    dot_general x1, matrix products, body(): jnp.einsum('htj,hsj->hts', grad_heads, value_heads, preferred_element_typ...  7.43 us
    dot_general x1, local copies, waits for them, and re-layouts, body(): jnp.einsum('htj,hsj->hts', grad_heads, value_heads, preferred_element_typ...  6.53 us
    dot_general x1, local copies, waits for them, and re-layouts, body(): jnp.einsum('htd,hsd->hts', query_heads, key_heads, preferred_element_type...  6.52 us
  transfers between devices with their start and end apart: 2, of which 2 were waited for; matrix products, arithmetic and copies ran while one was open for 17% of the time, Pallas kernels for 0%

commit v1 on v0

v1 whole, which is shorter than its diff:
```python
import functools

import jax
import jax.numpy as jnp
from jax import lax
from jax.experimental import pallas as pl
from jax.experimental.pallas import tpu as pltpu
from jax.sharding import PartitionSpec as P

DH = 128
norm_eps = 1e-06
MESH = pl.DeviceIdType.MESH
F32 = jnp.float32
BF16 = jnp.bfloat16


def mm(a, b):
    return lax.dot_general(a, b, (((1,), (0,)), ((), ())), preferred_element_type=F32)


def mm_nt(a, b):
    return lax.dot_general(a, b, (((1,), (1,)), ((), ())), preferred_element_type=F32)


def mm_tn(a, b):
    return lax.dot_general(a, b, (((0,), (0,)), ((), ())), preferred_element_type=F32)


def kernel(
    n_seq, n_head, q_hbm, k_hbm, v_hbm, gain_ref, og_hbm,
    out_hbm, gq_hbm, gk_hbm, gv_hbm, gg_ref,
    q, k, v, og, att, grad, stored, outv, gqv, gkv, gvv, gk_part, gv_part,
    own_f, own_b, xr_f, xr_b, zr_f, zr_b, zs_f, zs_b, ys_f, ys_b, yr_f, yr_b,
    state_bf, stats, stats_in, gain_parts, gain_in,
    load_sem, store_sem, send_f, recv_f, send_b, recv_b,
    head_send, head_recv, gain_send, gain_recv,
):
    me = lax.axis_index("seq")
    hd = lax.axis_index("head")
    rows, width = q.shape
    heads = width // DH
    half = heads // 2
    tile = rows // 2
    columns = width * n_head
    n_outer = n_seq // 2
    outer = me // 2
    inner = me % 2
    partner = me + 1 - 2 * inner
    n_levels = gain_in.shape[0]

    loads = [
        pltpu.make_async_copy(src, dst, load_sem.at[j])
        for j, (src, dst) in enumerate(((k_hbm, k), (v_hbm, v), (q_hbm, q), (og_hbm, og)))
    ]
    for copy in loads:
        copy.start()

    def level_peer(level):
        step = 2 ** level
        bit = (me // step) % 2
        return me + step - 2 * step * bit

    barrier = pltpu.get_barrier_semaphore()
    count = 0
    for r in range(1, n_head):
        pl.semaphore_signal(
            barrier, inc=1, device_id={"head": (hd + r) % n_head}, device_id_type=MESH)
        count += 1
    for level in range(n_levels):
        pl.semaphore_signal(
            barrier, inc=1, device_id={"seq": level_peer(level)}, device_id_type=MESH)
        count += 1

    odd = outer % 2
    third = outer - 1 + 2 * odd
    has_third = jnp.logical_and(third >= 0, third < n_outer)

    @pl.when(has_third)
    def _():
        pl.semaphore_signal(
            barrier, inc=1, device_id={"seq": 2 * third + inner}, device_id_type=MESH)

    def cols(h):
        return pl.ds(pl.multiple_of(h * DH, DH), DH)

    own_base = inner * half
    other_base = (1 - inner) * half

    def remote(src, dst, send, recv, peer):
        return pltpu.make_async_remote_copy(
            src_ref=src, dst_ref=dst, send_sem=send, recv_sem=recv,
            device_id=peer, device_id_type=MESH)

    class Scan:
        def __init__(self, reverse, own, xr, zr, zs, ys, yr, send, recv):
            self.own, self.xr, self.zr, self.zs, self.ys, self.yr = own, xr, zr, zs, ys, yr
            self.send, self.recv = send, recv
            self.at = n_outer - 1 - outer if reverse else outer
            self.side = 1 - inner if reverse else inner
            self.next = me - 2 if reverse else me + 2

        def x(self, j):
            return remote(self.own.at[other_base + j], self.xr.at[j],
                          self.send.at[0, j], self.recv.at[0, j], {"seq": partner})

        def z(self, j):
            return remote(self.zs.at[j], self.zr.at[j],
                          self.send.at[1, j], self.recv.at[1, j], {"seq": self.next})

        def y(self, j):
            return remote(self.ys.at[j], self.yr.at[j],
                          self.send.at[2, j], self.recv.at[2, j], {"seq": partner})

        def clear(self):
            @pl.when(self.at == 0)
            def _():
                self.zr[...] = jnp.zeros_like(self.zr)

        def step(self, j):
            self.x(j).wait_recv()

            @pl.when(self.at > 0)
            def _():
                self.z(j).wait_recv()

            before = self.zr[j]
            mine = self.own[own_base + j]
            theirs = self.xr[j]

            @pl.when(self.at < n_outer - 1)
            def _():
                self.zs[j] = before + (mine + theirs)
                self.z(j).start()

            self.ys[j] = jnp.where(self.side == 0, before + mine, before)
            self.y(j).start()
            return jnp.where(self.side == 0, before, before + theirs)

        def drain(self):
            def body(j, c):
                self.x(j).wait_send()
                self.y(j).wait_send()

                @pl.when(self.at < n_outer - 1)
                def _():
                    self.z(j).wait_send()
                return c
            lax.fori_loop(0, half, body, 0)

    fwd = Scan(False, own_f, xr_f, zr_f, zs_f, ys_f, yr_f, send_f, recv_f)
    bwd = Scan(True, own_b, xr_b, zr_b, zs_b, ys_b, yr_b, send_b, recv_b)
    fwd.clear()
    bwd.clear()

    loads[0].wait()
    loads[1].wait()
    own_f[other_base] = mm_tn(k[:, cols(other_base)], v[:, cols(other_base)])

    pl.semaphore_wait(barrier, jnp.where(has_third, count + 1, count))

    fwd.x(0).start()

    def first_states(j, c):
        h = other_base + j
        own_f[h] = mm_tn(k[:, cols(h)], v[:, cols(h)])
        fwd.x(j).start()
        return c
    lax.fori_loop(1, half, first_states, 0)

    def own_states(j, c):
        h = own_base + j
        own_f[h] = mm_tn(k[:, cols(h)], v[:, cols(h)])
        return c
    lax.fori_loop(0, half, own_states, 0)

    loads[2].wait()
    low = lax.broadcasted_iota(jnp.int32, (tile, tile), 0) >= lax.broadcasted_iota(
        jnp.int32, (tile, tile), 1)
    up = lax.broadcasted_iota(jnp.int32, (tile, tile), 0) <= lax.broadcasted_iota(
        jnp.int32, (tile, tile), 1)

    def keep(mask, x):
        return jnp.where(mask, x, 0.0).astype(BF16)

    def split(ref, h):
        return ref[0:tile, cols(h)], ref[tile:rows, cols(h)]

    def local_fwd(h):
        q0, q1 = split(q, h)
        k0, k1 = split(k, h)
        v0, v1 = split(v, h)
        att[0:tile, cols(h)] = mm(keep(low, mm_nt(q0, k0)), v0)
        att[tile:rows, cols(h)] = mm(mm_nt(q1, k0).astype(BF16), v0) + mm(
            keep(low, mm_nt(q1, k1)), v1)
        stored[h, 0] = keep(up, mm_nt(k0, q0))
        stored[h, 1] = mm_nt(k0, q1).astype(BF16)
        stored[h, 2] = keep(up, mm_nt(k1, q1))

    local_fwd(0)

    def chain_fwd(j, c):
        state_bf[own_base + j] = fwd.step(j).astype(BF16)
        local_fwd(1 + j)
        return c
    lax.fori_loop(0, half, chain_fwd, 0)

    def rest_fwd(h, c):
        local_fwd(h)
        return c
    lax.fori_loop(1 + half, heads, rest_fwd, 0)

    loads[3].wait()

    def attend(h, sums):
        square, dot = sums
        a = att[:, cols(h)] + mm(q[:, cols(h)], state_bf[h])
        att[:, cols(h)] = a
        scaled = og[:, cols(h)].astype(F32) * gain_ref[0:1, cols(h)]
        return square + a * a, dot + scaled * a

    def attend_own(j, sums):
        return attend(own_base + j, sums)

    def attend_other(j, sums):
        fwd.y(j).wait_recv()
        state_bf[other_base + j] = fwd.yr[j].astype(BF16)
        return attend(other_base + j, sums)

    zero = jnp.zeros((rows, DH), F32)
    sums = lax.fori_loop(0, half, attend_own, (zero, zero))
    square, dot = lax.fori_loop(0, half, attend_other, sums)
    lane = lax.broadcasted_iota(jnp.int32, (rows, DH), 1)
    both = jnp.where(lane == 0, jnp.sum(square, axis=1, keepdims=True),
                     jnp.sum(dot, axis=1, keepdims=True))
    stats[...] = jnp.transpose(both)[0:8, :]

    def head_copy(r):
        return remote(stats, stats_in.at[r - 1], head_send.at[r - 1], head_recv.at[r - 1],
                      {"head": (hd + r) % n_head})

    for r in range(1, n_head):
        head_copy(r).start()
    total = stats[...]
    for r in range(1, n_head):
        head_copy(r).wait_recv()
        total = total + stats_in[r - 1]
    total = jnp.transpose(jnp.concatenate([total] * (DH // 8), axis=0))
    inverse = lax.rsqrt(total[:, 0:1] / columns + norm_eps)
    dot_mean = total[:, 1:2] * inverse / columns

    def normalise(h):
        wide = og[:, cols(h)].astype(F32)
        gain = gain_ref[0:1, cols(h)]
        normed = att[:, cols(h)] * inverse
        outv[:, cols(h)] = (normed * gain).astype(BF16)
        part = (wide * normed).reshape(rows // 8, 8, DH)
        gain_parts[0, :, cols(h)] = jnp.sum(part, axis=0)
        g = (inverse * (wide * gain - normed * dot_mean)).astype(BF16)
        grad[:, cols(h)] = g
        own_b[h] = mm_tn(q[:, cols(h)], g)

    def norm_other(j, c):
        normalise(other_base + j)
        bwd.x(j).start()
        return c
    lax.fori_loop(0, half, norm_other, 0)

    def norm_own(j, c):
        normalise(own_base + j)
        return c
    lax.fori_loop(0, half, norm_own, 0)

    out_store = pltpu.make_async_copy(outv, out_hbm, store_sem.at[0])
    out_store.start()

    def gain_copy(level):
        return remote(gain_parts.at[level], gain_in.at[level], gain_send.at[level],
                      gain_recv.at[level], {"seq": level_peer(level)})

    gain_copy(0).start()

    def local_bwd(h):
        q0, q1 = split(q, h)
        k0, k1 = split(k, h)
        v0, v1 = split(v, h)
        g0, g1 = split(grad, h)
        state = state_bf[h]
        gqv[0:tile, cols(h)] = (
            mm_nt(g0, state) + mm(keep(low, mm_nt(g0, v0)), k0)).astype(BF16)
        gqv[tile:rows, cols(h)] = (
            mm_nt(g1, state) + mm(mm_nt(g1, v0).astype(BF16), k0)
            + mm(keep(low, mm_nt(g1, v1)), k1)).astype(BF16)
        gk_part[0:tile, cols(h)] = mm(keep(up, mm_nt(v0, g0)), q0) + mm(
            mm_nt(v0, g1).astype(BF16), q1)
        gk_part[tile:rows, cols(h)] = mm(keep(up, mm_nt(v1, g1)), q1)
        gv_part[0:tile, cols(h)] = mm(stored[h, 0], g0) + mm(stored[h, 1], g1)
        gv_part[tile:rows, cols(h)] = mm(stored[h, 2], g1)

    local_bwd(0)

    def chain_bwd(j, c):
        suffix = bwd.step(j).astype(BF16)
        state_bf[heads + own_base + j] = suffix
        local_bwd(1 + j)
        return c
    lax.fori_loop(0, half, chain_bwd, 0)

    for level in range(n_levels):
        gain_copy(level).wait_recv()
        new = gain_parts[level] + gain_in[level]
        gain_parts[level + 1] = new
        if level < n_levels - 1:
            gain_copy(level + 1).start()
        if 1 + half + level < heads:
            local_bwd(1 + half + level)
    gg_ref[...] = jnp.sum(gain_parts[n_levels], axis=0, keepdims=True)
    for h in range(1 + half + n_levels, heads):
        local_bwd(h)

    gq_store = pltpu.make_async_copy(gqv, gq_hbm, store_sem.at[1])
    gq_store.start()

    def finish(h):
        suffix = state_bf[heads + h]
        gkv[:, cols(h)] = (gk_part[:, cols(h)] + mm_nt(v[:, cols(h)], suffix)).astype(BF16)
        gvv[:, cols(h)] = (gv_part[:, cols(h)] + mm(k[:, cols(h)], suffix)).astype(BF16)

    def finish_own(j, c):
        finish(own_base + j)
        return c
    lax.fori_loop(0, half, finish_own, 0)

    span = half * DH
    own_cols = pl.ds(pl.multiple_of(own_base * DH, span), span)
    other_cols = pl.ds(pl.multiple_of(other_base * DH, span), span)
    stores = [
        pltpu.make_async_copy(src.at[:, c], dst.at[:, c], store_sem.at[2 + n])
        for n, (src, dst, c) in enumerate((
            (gkv, gk_hbm, own_cols), (gvv, gv_hbm, own_cols),
            (gkv, gk_hbm, other_cols), (gvv, gv_hbm, other_cols)))
    ]
    stores[0].start()
    stores[1].start()

    def finish_other(j, c):
        bwd.y(j).wait_recv()
        state_bf[heads + other_base + j] = bwd.yr[j].astype(BF16)
        finish(other_base + j)
        return c
    lax.fori_loop(0, half, finish_other, 0)
    stores[2].start()
    stores[3].start()

    fwd.drain()
    bwd.drain()
    for r in range(1, n_head):
        head_copy(r).wait_send()
    for level in range(n_levels):
        gain_copy(level).wait_send()
    out_store.wait()
    gq_store.wait()
    for copy in stores:
        copy.wait()


def body(n_seq, n_head, query_rows, key_rows, value_rows, norm_gain, out_grad):
    rows, width = query_rows.shape
    heads = width // DH
    half = heads // 2
    tile = rows // 2
    levels = n_seq.bit_length() - 1
    wide = jax.ShapeDtypeStruct((rows, width), BF16)
    vmem = pl.BlockSpec(memory_space=pltpu.VMEM)
    hbm = pl.BlockSpec(memory_space=pl.ANY)
    full = pltpu.VMEM((rows, width), BF16)
    full32 = pltpu.VMEM((rows, width), F32)
    half_states = pltpu.VMEM((half, DH, DH), F32)
    outs = pl.pallas_call(
        functools.partial(kernel, n_seq, n_head),
        out_shape=[wide] * 4 + [jax.ShapeDtypeStruct((1, width), F32)],
        in_specs=[hbm, hbm, hbm, vmem, hbm],
        out_specs=[hbm] * 4 + [vmem],
        scratch_shapes=[full, full, full, full, full32, full,
                        pltpu.VMEM((heads, 3, tile, tile), BF16),
                        full, full, full, full, full32, full32]
        + [pltpu.VMEM((heads, DH, DH), F32)] * 2
        + [half_states] * 10
        + [
            pltpu.VMEM((2 * heads, DH, DH), BF16),
            pltpu.VMEM((8, rows), F32),
            pltpu.VMEM((n_head - 1, 8, rows), F32),
            pltpu.VMEM((levels + 1, 8, width), F32),
            pltpu.VMEM((levels, 8, width), F32),
            pltpu.SemaphoreType.DMA((4,)),
            pltpu.SemaphoreType.DMA((6,)),
            pltpu.SemaphoreType.DMA((3, half)),
            pltpu.SemaphoreType.DMA((3, half)),
            pltpu.SemaphoreType.DMA((3, half)),
            pltpu.SemaphoreType.DMA((3, half)),
            pltpu.SemaphoreType.DMA((n_head - 1,)),
            pltpu.SemaphoreType.DMA((n_head - 1,)),
            pltpu.SemaphoreType.DMA((levels,)),
            pltpu.SemaphoreType.DMA((levels,)),
        ],
        compiler_params=pltpu.CompilerParams(
            collective_id=0, has_side_effects=True, vmem_limit_bytes=48 * 1024 * 1024),
    )(query_rows, key_rows, value_rows, norm_gain.reshape(1, width), out_grad)
    return (*outs[:4], outs[4].reshape(width))


def solution(mesh):
    in_specs = (P("seq", "head"), P("seq", "head"), P("seq", "head"), P("head"), P("seq", "head"))
    out_specs = (P("seq", "head"), P("seq", "head"), P("seq", "head"), P("seq", "head"), P("head"))
    return jax.shard_map(
        functools.partial(body, mesh.shape["seq"], mesh.shape["head"]),
        mesh=mesh, in_specs=in_specs, out_specs=out_specs, check_vma=False)
```

time: 230 us -> 67.1 us (0.29)
  waiting for transfers between devices: 87.1 us -> 0 us
  Pallas kernels: 0 us -> 58.9 us
  blocking collectives: 32.8 us -> 0 us
  matrix products: 31.5 us -> 0 us
  other arithmetic: 30.1 us -> 0 us
  local copies, waits for them, and re-layouts: 31.8 us -> 6.38 us
  between operations: 14.2 us -> 0.65 us
    all_gather x2 -> x0, waiting for transfers between devices: 87.1 us -> none  [prefix_2(): everything = lax.all_gather(array, axis)]
    pallas_call x0 -> x1, Pallas kernels: none -> 58.9 us  [body(): pl.pallas_call(functools.partial(kernel, n_seq, n_head), out_shape=[wide]...]
    psum x3 -> x0, blocking collectives: 32.8 us -> none  [the longest x1 20.4 us: body(): grad_gain = lax.psum(gain_part, 'seq')]
    dot_general x9 -> x0, matrix products: 31.5 us -> none  [the longest x1 7.43 us: body(): jnp.einsum('htj,hsj->hts', grad_heads, value_heads, preferred_element_typ...]
    select_n x16 -> x0, other arithmetic: 19.7 us -> none  [hop(): return jnp.where(reached, new, before)]
    dot_general x3 -> x0, local copies, waits for them, and re-layouts: 15.1 us -> none  [the longest x1 6.53 us: body(): jnp.einsum('htj,hsj->hts', grad_heads, value_heads, preferred_element_typ...]
    convert_element_type x3 -> x0, other arithmetic: 8.28 us -> none  [the longest x1 5.1 us: body(): scores_bf = jnp.where(causal, scores, 0.0).astype(jnp.bfloat16)]
    unnamed x20 -> x9, local copies, waits for them, and re-layouts: 12.2 us -> 6.38 us
  transfers between devices with their start and end apart: 2 -> 0, of which waited for: 2 -> 0; matrix products, arithmetic and copies ran while one was open for 17% -> 0% of each run, Pallas kernels for 0% -> 0%
where the time goes in v1:
time: 67.1 us; the launch traced here: 65.9 us
  Pallas kernels  58.9 us (88%)
  local copies, waits for them, and re-layouts  6.38 us (10%)
    pallas_call x1, Pallas kernels, body(): pl.pallas_call(functools.partial(kernel, n_seq, n_head), out_shape=[wide]...  58.9 us
    unnamed x9, local copies, waits for them, and re-layouts  6.38 us

profile of v1, /device:TPU:0, one launch (start us, length us, event | category | flops | bytes accessed | tf_op | source)
XLA Modules:
  0.0 65.9 jit_solution(3526928345730774693)
XLA Ops:
  0.6 0.0 copy-start
  0.6 1.2 %copy-done = bf16[512,1024]{1,0:T(8,128)(2,1)S(1)} copy-done((bf16[512,1024]{1,0:T(8,128)(2,1)S(1)}, bf16[512,1024]{1,0:T(8,128)(2,1)}, u32[]{:S(2)}) %copy-start) | copy-done | bytes 1048600
  1.9 0.0 copy-start.1
  1.9 0.7 %copy-done.1 = f32[1024]{0:T(1024)S(1)} copy-done((f32[1024]{0:T(1024)S(1)}, f32[1024]{0:T(1024)}, u32[]{:S(2)}) %copy-start.1) | copy-done | bytes 4120
  2.5 58.9 %shard_map.92 = (bf16[512,1024]{1,0:T(8,128)(2,1)S(1)}, bf16[512,1024]{1,0:T(8,128)(2,1)S(1)}, bf16[512,1024]{1,0:T(8,128)(2,1)S(1)}, bf16[512,1024]{1,0:T(8,128)(2,1)S(1)}, f32[1,1024]{1,0:T(1,128)S(1)}) custom-call(bf16[512,1024]{1,0:T(8,128)(2,1)S(1)} %copy-done, bf16[512,1024]{1,0:T(8,128)(2,1)} %k_hbm.1, bf16[512,1024]{1,0:T(8,128)(2,1)} %v_hbm.1, ...), custom_call_target="tpu_custom_call" | custom-call | tf_op jit(solution)/shard_map/pallas_call | solution.py:378
  61.5 1.0 %copy.15 = bf16[512,1024]{1,0:T(8,128)(2,1)} copy(bf16[512,1024]{1,0:T(8,128)(2,1)S(1)} %get-tuple-element.20) | data formatting | bytes 2097152
  62.4 1.0 %copy.16 = bf16[512,1024]{1,0:T(8,128)(2,1)} copy(bf16[512,1024]{1,0:T(8,128)(2,1)S(1)} %get-tuple-element.21) | data formatting | bytes 2097152
  63.4 1.0 %copy.17 = bf16[512,1024]{1,0:T(8,128)(2,1)} copy(bf16[512,1024]{1,0:T(8,128)(2,1)S(1)} %get-tuple-element.22) | data formatting | bytes 2097152
  64.4 1.0 %copy.18 = bf16[512,1024]{1,0:T(8,128)(2,1)} copy(bf16[512,1024]{1,0:T(8,128)(2,1)S(1)} %get-tuple-element.23) | data formatting | bytes 2097152
  65.3 0.6 copy.19
Async XLA Ops:
  0.6 1.2 %copy-start = (bf16[512,1024]{1,0:T(8,128)(2,1)S(1)}, bf16[512,1024]{1,0:T(8,128)(2,1)}, u32[]{:S(2)}) copy-start(bf16[512,1024]{1,0:T(8,128)(2,1)} %q_hbm.1) | copy-start | bytes 3145732
  1.9 0.7 %copy-start.1 = (f32[1024]{0:T(1024)S(1)}, f32[1024]{0:T(1024)}, u32[]{:S(2)}) copy-start(f32[1024]{0:T(1024)} %param.8) | copy-start | bytes 12292

commit v2 on v1

--- a/solution.py
+++ b/solution.py
@@ -8,6 +8,8 @@
 from jax.sharding import PartitionSpec as P
 
 DH = 128
+PARTS = 2
+PIECE = DH // PARTS
 norm_eps = 1e-06
 MESH = pl.DeviceIdType.MESH
 F32 = jnp.float32
@@ -27,9 +29,9 @@
 
 
 def kernel(
-    n_seq, n_head, q_hbm, k_hbm, v_hbm, gain_ref, og_hbm,
+    n_seq, n_head, q_hbm, k_hbm, v_hbm, gain_hbm, og_hbm,
     out_hbm, gq_hbm, gk_hbm, gv_hbm, gg_ref,
-    q, k, v, og, att, grad, stored, outv, gqv, gkv, gvv, gk_part, gv_part,
+    q, k, v, og, gain_ref, att, grad, stored, outv, gqv, gkv, gvv, gk_part, gv_part,
     own_f, own_b, xr_f, xr_b, zr_f, zr_b, zs_f, zs_b, ys_f, ys_b, yr_f, yr_b,
     state_bf, stats, stats_in, gain_parts, gain_in,
     load_sem, store_sem, send_f, recv_f, send_b, recv_b,
@@ -50,7 +52,8 @@
 
     loads = [
         pltpu.make_async_copy(src, dst, load_sem.at[j])
-        for j, (src, dst) in enumerate(((k_hbm, k), (v_hbm, v), (q_hbm, q), (og_hbm, og)))
+        for j, (src, dst) in enumerate((
+            (k_hbm, k), (v_hbm, v), (q_hbm, q), (og_hbm, og), (gain_hbm, gain_ref)))
     ]
     for copy in loads:
         copy.start()
@@ -99,51 +102,74 @@
             self.side = 1 - inner if reverse else inner
             self.next = me - 2 if reverse else me + 2
 
-        def x(self, j):
-            return remote(self.own.at[other_base + j], self.xr.at[j],
-                          self.send.at[0, j], self.recv.at[0, j], {"seq": partner})
-
-        def z(self, j):
-            return remote(self.zs.at[j], self.zr.at[j],
-                          self.send.at[1, j], self.recv.at[1, j], {"seq": self.next})
-
-        def y(self, j):
-            return remote(self.ys.at[j], self.yr.at[j],
-                          self.send.at[2, j], self.recv.at[2, j], {"seq": partner})
+        def x(self, j, p):
+            return remote(self.own.at[other_base + j, p], self.xr.at[j, p],
+                          self.send.at[0, j, p], self.recv.at[0, j, p], {"seq": partner})
+
+        def z(self, j, p):
+            return remote(self.zs.at[j, p], self.zr.at[j, p],
+                          self.send.at[1, j, p], self.recv.at[1, j, p], {"seq": self.next})
+
+        def y(self, j, p):
+            return remote(self.ys.at[j, p], self.yr.at[j, p],
+                          self.send.at[2, j, p], self.recv.at[2, j, p], {"seq": partner})
 
         def clear(self):
             @pl.when(self.at == 0)
             def _():
                 self.zr[...] = jnp.zeros_like(self.zr)
 
-        def step(self, j):
-            self.x(j).wait_recv()
+        def offer(self, j):
+            for p in range(PARTS):
+                self.x(j, p).start()
+
+        def step(self, j, p):
+            self.x(j, p).wait_recv()
 
             @pl.when(self.at > 0)
             def _():
-                self.z(j).wait_recv()
-
-            before = self.zr[j]
-            mine = self.own[own_base + j]
-            theirs = self.xr[j]
+                self.z(j, p).wait_recv()
+
+            before = self.zr[j, p]
+            mine = self.own[own_base + j, p]
+            theirs = self.xr[j, p]
 
             @pl.when(self.at < n_outer - 1)
             def _():
-                self.zs[j] = before + (mine + theirs)
-                self.z(j).start()
-
-            self.ys[j] = jnp.where(self.side == 0, before + mine, before)
-            self.y(j).start()
+                self.zs[j, p] = before + (mine + theirs)
+                self.z(j, p).start()
+
+            self.ys[j, p] = jnp.where(self.side == 0, before + mine, before)
+            self.y(j, p).start()
             return jnp.where(self.side == 0, before, before + theirs)
+
+        def chain(self, local, base, between, offset):
+            def body(j, c):
+                begin = jnp.where(j == 0, 0, jnp.minimum(heads, base + (j - 1) * between))
+                lax.fori_loop(begin, jnp.minimum(heads, base + j * between), local, 0)
+                for p in range(PARTS):
+                    state_bf[offset + own_base + j, p * PIECE:(p + 1) * PIECE] = self.step(
+                        j, p).astype(BF16)
+                return c
+            lax.fori_loop(0, half, body, 0)
+            return jnp.minimum(heads, base + (half - 1) * between)
+
+        def arrive(self, j, offset):
+            for p in range(PARTS):
+                self.y(j, p).wait_recv()
+                state_bf[offset + other_base + j, p * PIECE:(p + 1) * PIECE] = self.yr[
+                    j, p].astype(BF16)
 
         def drain(self):
             def body(j, c):
-                self.x(j).wait_send()
-                self.y(j).wait_send()
+                for p in range(PARTS):
+                    self.x(j, p).wait_send()
+                    self.y(j, p).wait_send()
 
                 @pl.when(self.at < n_outer - 1)
                 def _():
-                    self.z(j).wait_send()
+                    for p in range(PARTS):
+                        self.z(j, p).wait_send()
                 return c
             lax.fori_loop(0, half, body, 0)
 
@@ -154,22 +180,26 @@
 
     loads[0].wait()
     loads[1].wait()
-    own_f[other_base] = mm_tn(k[:, cols(other_base)], v[:, cols(other_base)])
+
+    def own_state(h):
+        own_f[h] = mm_tn(k[:, cols(h)], v[:, cols(h)]).reshape(PARTS, PIECE, DH)
+
+    own_state(other_base)
 
     pl.semaphore_wait(barrier, jnp.where(has_third, count + 1, count))
 
-    fwd.x(0).start()
+    fwd.offer(0)
 
     def first_states(j, c):
         h = other_base + j
-        own_f[h] = mm_tn(k[:, cols(h)], v[:, cols(h)])
-        fwd.x(j).start()
+        own_state(h)
+        fwd.offer(j)
         return c
     lax.fori_loop(1, half, first_states, 0)
 
     def own_states(j, c):
         h = own_base + j
-        own_f[h] = mm_tn(k[:, cols(h)], v[:, cols(h)])
+        own_state(h)
         return c
     lax.fori_loop(0, half, own_states, 0)
 
@@ -185,7 +215,7 @@
     def split(ref, h):
         return ref[0:tile, cols(h)], ref[tile:rows, cols(h)]
 
-    def local_fwd(h):
+    def local_fwd(h, c):
         q0, q1 = split(q, h)
         k0, k1 = split(k, h)
         v0, v1 = split(v, h)
@@ -195,21 +225,13 @@
         stored[h, 0] = keep(up, mm_nt(k0, q0))
         stored[h, 1] = mm_nt(k0, q1).astype(BF16)
         stored[h, 2] = keep(up, mm_nt(k1, q1))
-
-    local_fwd(0)
-
-    def chain_fwd(j, c):
-        state_bf[own_base + j] = fwd.step(j).astype(BF16)
-        local_fwd(1 + j)
-        return c
-    lax.fori_loop(0, half, chain_fwd, 0)
-
-    def rest_fwd(h, c):
-        local_fwd(h)
-        return c
-    lax.fori_loop(1 + half, heads, rest_fwd, 0)
+        return c
+
+    done = fwd.chain(local_fwd, 1 + 2 * fwd.at, 1, 0)
+    lax.fori_loop(done, heads, local_fwd, 0)
 
     loads[3].wait()
+    loads[4].wait()
 
     def attend(h, sums):
         square, dot = sums
@@ -222,8 +244,7 @@
         return attend(own_base + j, sums)
 
     def attend_other(j, sums):
-        fwd.y(j).wait_recv()
-        state_bf[other_base + j] = fwd.yr[j].astype(BF16)
+        fwd.arrive(j, 0)
         return attend(other_base + j, sums)
 
     zero = jnp.zeros((rows, DH), F32)
@@ -257,11 +278,11 @@
         gain_parts[0, :, cols(h)] = jnp.sum(part, axis=0)
         g = (inverse * (wide * gain - normed * dot_mean)).astype(BF16)
         grad[:, cols(h)] = g
-        own_b[h] = mm_tn(q[:, cols(h)], g)
+        own_b[h] = mm_tn(q[:, cols(h)], g).reshape(PARTS, PIECE, DH)
 
     def norm_other(j, c):
         normalise(other_base + j)
-        bwd.x(j).start()
+        bwd.offer(j)
         return c
     lax.fori_loop(0, half, norm_other, 0)
 
@@ -279,7 +300,7 @@
 
     gain_copy(0).start()
 
-    def local_bwd(h):
+    def local_bwd(h, c):
         q0, q1 = split(q, h)
         k0, k1 = split(k, h)
         v0, v1 = split(v, h)
@@ -295,27 +316,20 @@
         gk_part[tile:rows, cols(h)] = mm(keep(up, mm_nt(v1, g1)), q1)
         gv_part[0:tile, cols(h)] = mm(stored[h, 0], g0) + mm(stored[h, 1], g1)
         gv_part[tile:rows, cols(h)] = mm(stored[h, 2], g1)
-
-    local_bwd(0)
-
-    def chain_bwd(j, c):
-        suffix = bwd.step(j).astype(BF16)
-        state_bf[heads + own_base + j] = suffix
-        local_bwd(1 + j)
-        return c
-    lax.fori_loop(0, half, chain_bwd, 0)
-
-    for level in range(n_levels):
+        return c
+
+    def gain_level(level):
         gain_copy(level).wait_recv()
-        new = gain_parts[level] + gain_in[level]
-        gain_parts[level + 1] = new
+        gain_parts[level + 1] = gain_parts[level] + gain_in[level]
         if level < n_levels - 1:
             gain_copy(level + 1).start()
-        if 1 + half + level < heads:
-            local_bwd(1 + half + level)
-    gg_ref[...] = jnp.sum(gain_parts[n_levels], axis=0, keepdims=True)
-    for h in range(1 + half + n_levels, heads):
-        local_bwd(h)
+
+    last = bwd.at == n_outer - 1
+    done = bwd.chain(local_bwd, bwd.at, jnp.where(last, 1, 0), heads)
+    gain_level(0)
+    lax.fori_loop(done, heads, local_bwd, 0)
+    for level in range(1, min(2, n_levels)):
+        gain_level(level)
 
     gq_store = pltpu.make_async_copy(gqv, gq_hbm, store_sem.at[1])
     gq_store.start()
@@ -343,13 +357,16 @@
     stores[1].start()
 
     def finish_other(j, c):
-        bwd.y(j).wait_recv()
-        state_bf[heads + other_base + j] = bwd.yr[j].astype(BF16)
+        bwd.arrive(j, heads)
         finish(other_base + j)
         return c
     lax.fori_loop(0, half, finish_other, 0)
     stores[2].start()
     stores[3].start()
+
+    for level in range(2, n_levels):
+        gain_level(level)
+    gg_ref[...] = jnp.sum(gain_parts[n_levels], axis=0, keepdims=True)
 
     fwd.drain()
     bwd.drain()
@@ -360,6 +377,15 @@
     out_store.wait()
     gq_store.wait()
     for copy in stores:
+        copy.wait()
+
+
+def write_out(*refs):
+    sems = refs[10]
+    copies = [pltpu.make_async_copy(refs[n], refs[5 + n], sems.at[n]) for n in range(5)]
+    for copy in copies:
+        copy.start()
+    for copy in copies:
         copy.wait()
 
 
@@ -374,16 +400,16 @@
     hbm = pl.BlockSpec(memory_space=pl.ANY)
     full = pltpu.VMEM((rows, width), BF16)
     full32 = pltpu.VMEM((rows, width), F32)
-    half_states = pltpu.VMEM((half, DH, DH), F32)
+    half_states = pltpu.VMEM((half, PARTS, PIECE, DH), F32)
     outs = pl.pallas_call(
         functools.partial(kernel, n_seq, n_head),
         out_shape=[wide] * 4 + [jax.ShapeDtypeStruct((1, width), F32)],
-        in_specs=[hbm, hbm, hbm, vmem, hbm],
+        in_specs=[hbm] * 5,
         out_specs=[hbm] * 4 + [vmem],
-        scratch_shapes=[full, full, full, full, full32, full,
+        scratch_shapes=[full, full, full, full, pltpu.VMEM((1, width), F32), full32, full,
                         pltpu.VMEM((heads, 3, tile, tile), BF16),
                         full, full, full, full, full32, full32]
-        + [pltpu.VMEM((heads, DH, DH), F32)] * 2
+        + [pltpu.VMEM((heads, PARTS, PIECE, DH), F32)] * 2
         + [half_states] * 10
         + [
             pltpu.VMEM((2 * heads, DH, DH), BF16),
@@ -391,12 +417,12 @@
             pltpu.VMEM((n_head - 1, 8, rows), F32),
             pltpu.VMEM((levels + 1, 8, width), F32),
             pltpu.VMEM((levels, 8, width), F32),
-            pltpu.SemaphoreType.DMA((4,)),
+            pltpu.SemaphoreType.DMA((5,)),
             pltpu.SemaphoreType.DMA((6,)),
-            pltpu.SemaphoreType.DMA((3, half)),
-            pltpu.SemaphoreType.DMA((3, half)),
-            pltpu.SemaphoreType.DMA((3, half)),
-            pltpu.SemaphoreType.DMA((3, half)),
+            pltpu.SemaphoreType.DMA((3, half, PARTS)),
+            pltpu.SemaphoreType.DMA((3, half, PARTS)),
+            pltpu.SemaphoreType.DMA((3, half, PARTS)),
+            pltpu.SemaphoreType.DMA((3, half, PARTS)),
             pltpu.SemaphoreType.DMA((n_head - 1,)),
             pltpu.SemaphoreType.DMA((n_head - 1,)),
             pltpu.SemaphoreType.DMA((levels,)),
@@ -405,6 +431,14 @@
         compiler_params=pltpu.CompilerParams(
             collective_id=0, has_side_effects=True, vmem_limit_bytes=48 * 1024 * 1024),
     )(query_rows, key_rows, value_rows, norm_gain.reshape(1, width), out_grad)
+    outs = pl.pallas_call(
+        write_out,
+        out_shape=[jax.ShapeDtypeStruct(o.shape, o.dtype) for o in outs],
+        in_specs=[hbm] * 5,
+        out_specs=[hbm] * 5,
+        scratch_shapes=[pltpu.SemaphoreType.DMA((5,))],
+        compiler_params=pltpu.CompilerParams(vmem_limit_bytes=1024 * 1024),
+    )(*outs)
     return (*outs[:4], outs[4].reshape(width))
 
 

time: 67.1 us -> 56.6 us (0.84); the launches traced: 65.9 us -> 56.4 us
  Pallas kernels: 58.9 us -> 53.9 us
  local copies, waits for them, and re-layouts: 6.38 us -> 1.9 us
    pallas_call x1, Pallas kernels: 58.9 us -> 51.8 us  [body(): pl.pallas_call(functools.partial(kernel, n_seq, n_head), out_shape=[wide]...]
    unnamed x9 -> x4, local copies, waits for them, and re-layouts: 6.38 us -> 1.9 us
    pallas_call x0 -> x1, Pallas kernels: none -> 2.05 us  [body(): pl.pallas_call(write_out, out_shape=[jax.ShapeDtypeStruct(o.shape, o.dtyp...]
where the time goes in v2:
time: 56.6 us; the launch traced here: 56.4 us
  Pallas kernels  53.9 us (95%)
  local copies, waits for them, and re-layouts  1.9 us (3%)
  between operations  0.65 us (1%)
    pallas_call x1, Pallas kernels, body(): pl.pallas_call(functools.partial(kernel, n_seq, n_head), out_shape=[wide]...  51.8 us
    pallas_call x1, Pallas kernels, body(): pl.pallas_call(write_out, out_shape=[jax.ShapeDtypeStruct(o.shape, o.dtyp...  2.05 us
    unnamed x4, local copies, waits for them, and re-layouts  1.9 us

profile of v2, /device:TPU:0, one launch (start us, length us, event | category | flops | bytes accessed | tf_op | source)
XLA Modules:
  0.0 56.4 jit_solution(11751335427782377262)
XLA Ops:
  0.6 0.0 copy-start
  0.6 1.2 %copy-done = bf16[512,1024]{1,0:T(8,128)(2,1)S(1)} copy-done((bf16[512,1024]{1,0:T(8,128)(2,1)S(1)}, bf16[512,1024]{1,0:T(8,128)(2,1)}, u32[]{:S(2)}) %copy-start) | copy-done | bytes 1048600
  1.9 0.0 copy-start.1
  1.9 0.7 %copy-done.1 = f32[1024]{0:T(1024)S(1)} copy-done((f32[1024]{0:T(1024)S(1)}, f32[1024]{0:T(1024)}, u32[]{:S(2)}) %copy-start.1) | copy-done | bytes 4120
  2.5 51.8 %shard_map.92 = (bf16[512,1024]{1,0:T(8,128)(2,1)S(1)}, bf16[512,1024]{1,0:T(8,128)(2,1)S(1)}, bf16[512,1024]{1,0:T(8,128)(2,1)S(1)}, bf16[512,1024]{1,0:T(8,128)(2,1)S(1)}, f32[1,1024]{1,0:T(1,128)S(1)}) custom-call(bf16[512,1024]{1,0:T(8,128)(2,1)S(1)} %copy-done, bf16[512,1024]{1,0:T(8,128)(2,1)} %k_hbm.1, bf16[512,1024]{1,0:T(8,128)(2,1)} %v_hbm.1, ...), custom_call_target="tpu_custom_call" | custom-call | tf_op jit(solution)/shard_map/pallas_call | solution.py:404
  54.4 2.1 %shard_map.93 = (bf16[512,1024]{1,0:T(8,128)(2,1)}, bf16[512,1024]{1,0:T(8,128)(2,1)}, bf16[512,1024]{1,0:T(8,128)(2,1)}, bf16[512,1024]{1,0:T(8,128)(2,1)}, f32[1,1024]{1,0:T(1,128)}) custom-call(bf16[512,1024]{1,0:T(8,128)(2,1)S(1)} %get-tuple-element.15.refs_0_, bf16[512,1024]{1,0:T(8,128)(2,1)S(1)} %get-tuple-element.16.refs_1_, ...), custom_call_target="tpu_custom_call" | custom-call | tf_op jit(solution)/shard_map/pallas_call | solution.py:434
Async XLA Ops:
  0.6 1.2 %copy-start = (bf16[512,1024]{1,0:T(8,128)(2,1)S(1)}, bf16[512,1024]{1,0:T(8,128)(2,1)}, u32[]{:S(2)}) copy-start(bf16[512,1024]{1,0:T(8,128)(2,1)} %q_hbm.1) | copy-start | bytes 3145732
  1.9 0.7 %copy-start.1 = (f32[1024]{0:T(1024)S(1)}, f32[1024]{0:T(1024)}, u32[]{:S(2)}) copy-start(f32[1024]{0:T(1024)} %param.8) | copy-start | bytes 12292
